TPU v7x, 32 devices: a whole 2x2x4 slice. The times are simulated.
32 devices in a mesh: pipe: 4 (over y, core), seq: 8 (over z, x).
Axes of the slice: x: 2, y: 2, z: 4, core: 2. Of those that a mesh axis runs over, the one named last changes fastest.
Arguments:
- queries: bfloat16 [4, 2048, 4096], P('pipe', 'seq'), may hold values from -50 to 50
- keys: bfloat16 [4, 2048, 512], P('pipe', 'seq'), may hold values from -4 to 4
- values: bfloat16 [4, 2048, 512], P('pipe', 'seq'), may hold values from -6 to 6
- out_grad: bfloat16 [4, 2048, 4096], P('pipe', 'seq'), may hold values from -96 to 96
- global_blocks: int32 [4, 32, 2], P('pipe'), may hold values from 0 to 15
- random_blocks: int32 [4, 32, 16, 3], P('pipe'), may hold values from 0 to 15
Outputs:
- query_grad: bfloat16 [4, 2048, 4096], P('pipe', 'seq')
- key_grad: bfloat16 [4, 2048, 512], P('pipe', 'seq')
- value_grad: bfloat16 [4, 2048, 512], P('pipe', 'seq')
- incoming_query: bfloat16 [4, 2048, 4096], P('pipe', 'seq')
- incoming_key: bfloat16 [4, 2048, 512], P('pipe', 'seq')
- incoming_value: bfloat16 [4, 2048, 512], P('pipe', 'seq')
All inputs are finite; a program needn't handle non-finite values.
Results may differ from a plain program's by a relative error of at most 0.0086.
Values may be sent and summed in bfloat16 or wider, within the bound.
A program may use at most 256 MiB of HBM per device.

v0:
```python
import jax
import jax.numpy as jnp
from jax import lax
from jax.sharding import PartitionSpec as P

HEADS = 32
KV_HEADS = 4
HEAD = 128
BLOCK = 128


def from_behind(value, axis, by):
    size = lax.axis_size(axis)
    pairs = [(i, i + by) for i in range(size) if 0 <= i + by < size]
    return lax.ppermute(value, axis, pairs)


def backward_tiles(
    query_rows, grad_rows, key_source, value_source, global_rows, random_rows, first
):
    heads_here, local_blocks, block, width = query_rows.shape
    sources = key_source.shape[0]
    total_blocks = key_source.shape[1]
    ratio = heads_here // sources
    span = min(4, local_blocks)
    groups = local_blocks // span
    steps = heads_here * groups
    nglob = global_rows.shape[1]
    nrand = random_rows.shape[2]
    scale = width ** (-0.5)
    stride = total_blocks + 2
    picks = (
        random_rows.reshape(sources, -1)[:, :, None]
        == jnp.arange(total_blocks, dtype=jnp.int32)[None, None, :]
    ).astype(jnp.bfloat16)

    def select(source):
        flat = source.reshape(sources, total_blocks, block * width)
        chosen = jnp.einsum("sra,sab->srb", picks, flat, preferred_element_type=jnp.float32).astype(
            jnp.bfloat16
        )
        return chosen.reshape(steps, span * nrand, block, width)

    def wrap_pad(source):
        return jnp.concatenate([source[:, -1:], source, source[:, :1]], axis=1).reshape(
            sources * stride, block, width
        )

    key_pad = wrap_pad(key_source)
    value_pad = wrap_pad(value_source)
    rand_keys = select(key_source)
    rand_values = select(value_source)
    glob_steps = jnp.repeat(global_rows, groups, axis=0)

    def step(totals, inputs):
        query_group, grad_group, key_extra, value_extra, glob, index = inputs
        head = index // groups
        base = head // ratio * stride
        start = base + first + index % groups * span
        glob_at = base + glob + 1

        def tiles(padded, extra):
            parts = [
                lax.dynamic_slice_in_dim(padded, start + offset, span, 0)[:, None]
                for offset in range(3)
            ]
            for slot in range(nglob):
                single = lax.dynamic_slice_in_dim(padded, glob_at[slot], 1, 0)[None]
                parts.append(jnp.broadcast_to(single, (span, 1, block, width)))
            parts.append(extra.reshape(span, nrand, block, width))
            return jnp.concatenate(parts, axis=1).reshape(span, -1, width)

        key_tiles = tiles(key_pad, key_extra)
        value_tiles = tiles(value_pad, value_extra)
        scores = (
            jnp.einsum("gqd,gkd->gqk", query_group, key_tiles, preferred_element_type=jnp.float32)
            * scale
        )
        shifted = jnp.exp(scores - jnp.max(scores, axis=-1, keepdims=True))
        weights = shifted / jnp.sum(shifted, axis=-1, keepdims=True)
        weights_low = weights.astype(jnp.bfloat16)
        output = jnp.einsum(
            "gqk,gkd->gqd", weights_low, value_tiles, preferred_element_type=jnp.float32
        )
        row_dot = jnp.sum(grad_group.astype(jnp.float32) * output, axis=-1, keepdims=True)
        grad_weights = jnp.einsum(
            "gqd,gkd->gqk", grad_group, value_tiles, preferred_element_type=jnp.float32
        )
        grad_scores = (weights * (grad_weights - row_dot) * scale).astype(jnp.bfloat16)
        grad_query = jnp.einsum(
            "gqk,gkd->gqd", grad_scores, key_tiles, preferred_element_type=jnp.float32
        )
        key_terms = jnp.einsum(
            "gqk,gqd->gkd", grad_scores, query_group, preferred_element_type=jnp.float32
        ).reshape(span, -1, block, width)
        value_terms = jnp.einsum(
            "gqk,gqd->gkd", weights_low, grad_group, preferred_element_type=jnp.float32
        ).reshape(span, -1, block, width)

        def accumulate(total, terms):
            for offset in range(3):
                current = lax.dynamic_slice_in_dim(total, start + offset, span, 0)
                total = lax.dynamic_update_slice_in_dim(
                    total, current + terms[:, offset], start + offset, 0
                )
            for slot in range(nglob):
                current = lax.dynamic_slice_in_dim(total, glob_at[slot], 1, 0)
                summed = jnp.sum(terms[:, 3 + slot], axis=0, keepdims=True)
                total = lax.dynamic_update_slice_in_dim(total, current + summed, glob_at[slot], 0)
            rest = terms[:, 3 + nglob :]
            upper = rest.astype(jnp.bfloat16)
            lower = (rest - upper.astype(jnp.float32)).astype(jnp.bfloat16)
            return (total, upper, lower)

        key_total, key_upper, key_lower = accumulate(totals[0], key_terms)
        value_total, value_upper, value_lower = accumulate(totals[1], value_terms)
        return (
            (key_total, value_total),
            (grad_query, key_upper, key_lower, value_upper, value_lower),
        )

    zeros_total = jnp.zeros((sources * stride, block, width), jnp.float32)
    inputs = (
        query_rows.reshape(steps, span, block, width),
        grad_rows.reshape(steps, span, block, width),
        rand_keys,
        rand_values,
        glob_steps,
        jnp.arange(steps, dtype=jnp.int32),
    )
    totals, outputs = lax.scan(step, (zeros_total, zeros_total), inputs)
    grad_query, key_upper, key_lower, value_upper, value_lower = outputs

    def finish(total, upper, lower):
        total = total.reshape(sources, stride, block, width)
        main = total[:, 1 : total_blocks + 1]
        main = main.at[:, 0].add(total[:, stride - 1]).at[:, total_blocks - 1].add(total[:, 0])
        spread = jnp.einsum(
            "sra,srb->sab",
            picks,
            upper.reshape(sources, -1, block * width),
            preferred_element_type=jnp.float32,
        )
        spread = spread + jnp.einsum(
            "sra,srb->sab",
            picks,
            lower.reshape(sources, -1, block * width),
            preferred_element_type=jnp.float32,
        )
        return main + spread.reshape(sources, total_blocks, block, width)

    return (
        grad_query.reshape(heads_here, local_blocks, block, width),
        finish(totals[0], key_upper, key_lower),
        finish(totals[1], value_upper, value_lower),
    )


def body(queries, keys, values, out_grad, global_blocks, random_blocks):
    query_here = queries[0]
    tokens = query_here.shape[0]
    devices = lax.axis_size("seq")
    device = lax.axis_index("seq")
    total_blocks = tokens * devices // BLOCK
    per_device = HEADS // devices
    group_size = HEADS // KV_HEADS
    global_rows = global_blocks[0]
    random_rows = random_blocks[0]

    def spread(matrix):
        return matrix.reshape(tokens, devices, per_device, HEAD).transpose(2, 0, 1, 3)

    def widen(matrix):
        shaped = matrix.reshape(tokens, KV_HEADS, 1, HEAD)
        return jnp.broadcast_to(shaped, (tokens, KV_HEADS, group_size, HEAD)).reshape(
            tokens, HEADS * HEAD
        )

    query_heads, key_heads, value_heads, grad_heads = (
        lax.all_to_all(spread(query_here), "seq", split_axis=2, concat_axis=1, tiled=True),
        lax.all_to_all(spread(widen(keys[0])), "seq", split_axis=2, concat_axis=1, tiled=True),
        lax.all_to_all(spread(widen(values[0])), "seq", split_axis=2, concat_axis=1, tiled=True),
        lax.all_to_all(spread(out_grad[0]), "seq", split_axis=2, concat_axis=1, tiled=True),
    )

    def as_tiles(matrix):
        return matrix.reshape(per_device, total_blocks, BLOCK, HEAD)

    my_global = lax.dynamic_slice_in_dim(global_rows, device * per_device, per_device, 0)
    my_random = lax.dynamic_slice_in_dim(random_rows, device * per_device, per_device, 0)
    grad_query, key_total, value_total = backward_tiles(
        as_tiles(query_heads),
        as_tiles(grad_heads),
        as_tiles(key_heads),
        as_tiles(value_heads),
        my_global,
        my_random,
        0,
    )
    query_back = lax.all_to_all(
        grad_query.astype(jnp.bfloat16).reshape(per_device, tokens * devices, 1, HEAD),
        "seq",
        split_axis=1,
        concat_axis=2,
        tiled=True,
    )
    query_grad = query_back.transpose(1, 2, 0, 3).reshape(tokens, HEADS * HEAD)
    key_back, value_back = (
        lax.all_to_all(
            key_total.reshape(per_device, tokens * devices, 1, HEAD),
            "seq",
            split_axis=1,
            concat_axis=2,
            tiled=True,
        ),
        lax.all_to_all(
            value_total.reshape(per_device, tokens * devices, 1, HEAD),
            "seq",
            split_axis=1,
            concat_axis=2,
            tiled=True,
        ),
    )

    def fold_heads(matrix):
        return jnp.sum(
            matrix.transpose(1, 2, 0, 3).reshape(tokens, KV_HEADS, group_size, HEAD), axis=2
        ).reshape(tokens, KV_HEADS * HEAD)

    key_grad = fold_heads(key_back)
    value_grad = fold_heads(value_back)
    query_grad = query_grad[None]
    key_grad = key_grad.astype(jnp.bfloat16)[None]
    value_grad = value_grad.astype(jnp.bfloat16)[None]
    incoming_query, incoming_key, incoming_value = from_behind(
        (query_grad, key_grad, value_grad), "pipe", -1
    )
    return (query_grad, key_grad, value_grad, incoming_query, incoming_key, incoming_value)


def solution(mesh):
    in_specs = (
        P("pipe", "seq", None),
        P("pipe", "seq", None),
        P("pipe", "seq", None),
        P("pipe", "seq", None),
        P("pipe", None, None),
        P("pipe", None, None, None),
    )
    out_specs = (
        P("pipe", "seq", None),
        P("pipe", "seq", None),
        P("pipe", "seq", None),
        P("pipe", "seq", None),
        P("pipe", "seq", None),
        P("pipe", "seq", None),
    )
    return jax.shard_map(body, mesh=mesh, in_specs=in_specs, out_specs=out_specs, check_vma=False)
```

profile of v0, /device:TPU:1, one launch (start us, length us, event | category | flops | bytes accessed | tf_op | source)
XLA Modules:
  0.0 1175.0 jit_solution(3175582534563470422)
XLA Ops:
  3.6 6.4 all-to-all-start.1
  10.1 47.3 %all-to-all-done.1 = bf16[4,256,8,128]{3,1,0,2:T(8,128)(2,1)S(1)} async-done(((bf16[4,256,8,128]{3,1,0,2:T(8,128)(2,1)}), bf16[4,256,8,128]{3,1,0,2:T(8,128)(2,1)S(1)}, u32[]{:S(2)}, u32[]{:S(2)}) %all-to-all-start.1) | async-done | bytes 2097184 | tf_op jit(solution)/shard_map/all_to_all | solution.py:181
  59.3 4.7 all-to-all-start.3
  72.0 39.1 %all-to-all-done.3 = bf16[4,256,8,128]{3,1,0,2:T(8,128)(2,1)} async-done(((bf16[4,256,8,128]{3,1,0,2:T(8,128)(2,1)}), bf16[4,256,8,128]{3,1,0,2:T(8,128)(2,1)}, u32[]{:S(2)}, u32[]{:S(2)}) %all-to-all-start.3) | async-done | bytes 2097184 | tf_op jit(solution)/shard_map/all_to_all | solution.py:182
  111.0 5.1 all-to-all-start
  124.2 39.6 %all-to-all-done = bf16[4,256,8,128]{3,1,0,2:T(8,128)(2,1)S(1)} async-done(((bf16[4,256,8,128]{3,1,0,2:T(8,128)(2,1)}), bf16[4,256,8,128]{3,1,0,2:T(8,128)(2,1)S(1)}, u32[]{:S(2)}, u32[]{:S(2)}) %all-to-all-start) | async-done | bytes 2097184 | tf_op jit(solution)/shard_map/all_to_all | solution.py:180
  199.2 16.1 %all-to-all-done.2 = bf16[4,256,8,128]{3,1,0,2:T(8,128)(2,1)} async-done(((bf16[4,256,8,128]{3,1,0,2:T(8,128)(2,1)}), bf16[4,256,8,128]{3,1,0,2:T(8,128)(2,1)}, u32[]{:S(2)}, u32[]{:S(2)}) %all-to-all-start.2) | async-done | bytes 2097184 | tf_op jit(solution)/shard_map/all_to_all | solution.py:183
  223.9 673.4 %while.29 = (s32[]{:T(128)}, f32[72,128,128]{2,1,0:T(8,128)}, f32[72,128,128]{2,1,0:T(8,128)}, bf16[16,4,128,128]{3,2,1,0:T(8,128)(2,1)}, bf16[16,4,3,128,128]{4...) while((s32[]{:T(128)}, f32[72,128,128]{2,1,0:T(8,128)}, ...), condition=%wide.region_8.9_spmd, body=%wide.region_0.8_spmd.sunk | while | flops 814023232 | bytes 37240592 | solution.py:131
  897.3 4.6 copy.143
  901.9 5.5 all-to-all-start.4
  912.1 10.3 reshape.348
  922.3 10.3 reshape.349
  943.5 4.7 copy.148
  948.3 6.1 all-to-all-done.4
  954.3 5.4 all-to-all-start.6
  959.7 4.8 slice.280
  964.5 10.3 reshape.343
  974.8 10.3 reshape.344
  996.0 4.7 copy.146
  1000.7 50.7 %all-to-all-done.6 = f32[4,2048,1,128]{3,0,2,1:T(4,128)} async-done(((f32[4,2048,1,128]{3,0,2,1:T(4,128)}), f32[4,2048,1,128]{3,0,2,1:T(4,128)}, u32[]{:S(2)}, u32[]{:S(2)}) %all-to-all-start.6) | async-done | bytes 4194336 | tf_op jit(solution)/shard_map/all_to_all | solution.py:216
  1051.4 5.4 all-to-all-start.5
  1064.9 9.5 reduce_sum.123
  1077.2 71.4 %all-to-all-done.5 = f32[4,2048,1,128]{3,0,2,1:T(4,128)} async-done(((f32[4,2048,1,128]{3,0,2,1:T(4,128)}), f32[4,2048,1,128]{3,0,2,1:T(4,128)}, u32[]{:S(2)}, u32[]{:S(2)}) %all-to-all-start.5) | async-done | bytes 4194336 | tf_op jit(solution)/shard_map/all_to_all | solution.py:209
  1148.5 9.2 reduce_sum.118
  (690 shorter events, 686.1 us)
Async XLA Ops:
  0.6 167.6 %copy-start = (s32[1,32,16,3]{1,2,3,0:T(8,128)S(1)}, s32[1,32,16,3]{1,2,3,0:T(8,128)}, u32[]{:S(2)}) copy-start(s32[1,32,16,3]{1,2,3,0:T(8,128)} %param.21) | copy-start | bytes 18436
  1.7 8.3 copy-start.11
  3.6 53.7 %all-to-all-start.1 = ((bf16[4,256,8,128]{3,1,0,2:T(8,128)(2,1)}), bf16[4,256,8,128]{3,1,0,2:T(8,128)(2,1)S(1)}, u32[]{:S(2)}, u32[]{:S(2)}) async-start(bf16[4,256,8,128]{3,1,0,2:T(8,128)(2,1)} %transpose.47), calls=%async_computation.1 | async-start | bytes 4194304 | tf_op jit(solution)/shard_map/all_to_all | solution.py:181
  57.3 10.7 copy-start.8
  59.3 51.7 %all-to-all-start.3 = ((bf16[4,256,8,128]{3,1,0,2:T(8,128)(2,1)}), bf16[4,256,8,128]{3,1,0,2:T(8,128)(2,1)}, u32[]{:S(2)}, u32[]{:S(2)}) async-start(bf16[4,256,8,128]{3,1,0,2:T(8,128)(2,1)} %transpose.49), calls=%async_computation.3 | async-start | bytes 4194304 | tf_op jit(solution)/shard_map/all_to_all | solution.py:182
  111.0 52.7 %all-to-all-start = ((bf16[4,256,8,128]{3,1,0,2:T(8,128)(2,1)}), bf16[4,256,8,128]{3,1,0,2:T(8,128)(2,1)S(1)}, u32[]{:S(2)}, u32[]{:S(2)}) async-start(bf16[4,256,8,128]{3,1,0,2:T(8,128)(2,1)} %copy.133), calls=%async_computation | async-start | bytes 4194304 | tf_op jit(solution)/shard_map/all_to_all | solution.py:180
  120.2 48.4 %copy-start.12 = (s32[1,32,2]{1,2,0:T(2,128)S(1)}, s32[1,32,2]{1,2,0:T(2,128)}, u32[]{:S(2)}) copy-start(s32[1,32,2]{1,2,0:T(2,128)} %param.20) | copy-start | bytes 772
  163.7 5.1 copy-start.9
  163.7 51.5 %all-to-all-start.2 = ((bf16[4,256,8,128]{3,1,0,2:T(8,128)(2,1)}), bf16[4,256,8,128]{3,1,0,2:T(8,128)(2,1)}, u32[]{:S(2)}, u32[]{:S(2)}) async-start(bf16[4,256,8,128]{3,1,0,2:T(8,128)(2,1)} %copy.139), calls=%async_computation.2 | async-start | bytes 4194304 | tf_op jit(solution)/shard_map/all_to_all | solution.py:183
  170.6 6.1 copy-start.4
  188.9 4.6 copy-start.10
  193.4 2.3 copy-start.5
  901.9 52.4 %all-to-all-start.4 = ((bf16[4,2048,1,128]{3,0,2,1:T(4,128)(2,1)}), bf16[4,2048,1,128]{3,0,2,1:T(4,128)(2,1)S(1)}, u32[]{:S(2)}, u32[]{:S(2)}) async-start(bf16[4,2048,1,128]{3,0,2,1:T(4,128)(2,1)} %copy.143), calls=%async_computation.4 | async-start | bytes 4194304 | tf_op jit(solution)/shard_map/all_to_all | solution.py:200
  932.6 4.6 copy-start.3
  938.2 2.2 copy-start.7
  954.3 97.1 %all-to-all-start.6 = ((f32[4,2048,1,128]{3,0,2,1:T(4,128)}), f32[4,2048,1,128]{3,0,2,1:T(4,128)}, u32[]{:S(2)}, u32[]{:S(2)}) async-start(f32[4,2048,1,128]{3,0,2,1:T(4,128)} %bitcast.344), calls=%async_computation.6 | async-start | bytes 8388608 | tf_op jit(solution)/shard_map/all_to_all | solution.py:216
  985.1 4.6 copy-start.2
  990.6 2.2 copy-start.6
  1051.4 97.1 %all-to-all-start.5 = ((f32[4,2048,1,128]{3,0,2,1:T(4,128)}), f32[4,2048,1,128]{3,0,2,1:T(4,128)}, u32[]{:S(2)}, u32[]{:S(2)}) async-start(f32[4,2048,1,128]{3,0,2,1:T(4,128)} %bitcast.345), calls=%async_computation.5 | async-start | bytes 8388608 | tf_op jit(solution)/shard_map/all_to_all | solution.py:209
  1061.2 104.0 %collective-permute-start = (bf16[1,256,4096]{1,2,0:T(8,128)(2,1)S(1)}, bf16[1,256,4096]{1,2,0:T(8,128)(2,1)}, u32[]{:S(2)}, u32[]{:S(2)}) collective-permute-start(bf16[1,256,4096]{1,2,0:T(8,128)(2,1)S(1)} %bitcast.350), channel_id=1, source_target_pairs={{8,0},{16,8},{24,16},{9,1},{17,9},{25,17},{10,2},{18,10},{26,18},{... | collective-permute-start | bytes 6291464 | tf_op jit(solution)/shard_map/ppermute | solution.py:15
  1075.2 96.7 %collective-permute-start.2 = (bf16[1,256,512]{1,2,0:T(8,128)(2,1)}, bf16[1,256,512]{1,2,0:T(8,128)(2,1)}, u32[]{:S(2)}, u32[]{:S(2)}) collective-permute-start(bf16[1,256,512]{1,2,0:T(8,128)(2,1)} %bitcast.78), channel_id=1, source_target_pairs={{8,0},{16,8},{24,16},{9,1},{17,9},{25,17},{10,2},{18,10},{26,18},{... | collective-permute-start | bytes 786440 | tf_op jit(solution)/shard_map/ppermute | solution.py:15
  1158.0 15.8 %collective-permute-start.1 = (bf16[1,256,512]{1,2,0:T(8,128)(2,1)S(1)}, bf16[1,256,512]{1,2,0:T(8,128)(2,1)S(1)}, u32[]{:S(2)}, u32[]{:S(2)}) collective-permute-start(bf16[1,256,512]{1,2,0:T(8,128)(2,1)S(1)} %bitcast.362), channel_id=1, source_target_pairs={{8,0},{16,8},{24,16},{9,1},{17,9},{25,17},{10,2},{18,10},{26,18},{... | collective-permute-start | bytes 786440 | tf_op jit(solution)/shard_map/ppermute | solution.py:15
  1162.4 12.2 %copy-start.1 = (s32[1,32,16,3]{1,2,3,0:T(8,128)S(1)}, s32[1,32,16,3]{1,2,3,0:T(8,128)}, u32[]{:S(2)}) copy-start(s32[1,32,16,3]{1,2,3,0:T(8,128)} %param.21) | copy-start | bytes 18436
where the time goes:
time: 1200 us; the launch traced here: 1180 us
  local copies, waits for them, and re-layouts  307 us (26%)
  other arithmetic  286 us (24%)
  waiting for transfers between devices  270 us (22%)
  matrix products  158 us (13%)
  loops' own time  106 us (9%)
  starting transfers between devices  46.8 us (4%)
    dynamic_update_slice x80, other arithmetic, accumulate(): lax.dynamic_update_slice_in_dim(total, current + terms[:, offset], start...  138 us
    another operation x1, loops' own time, backward_tiles(): totals, outputs = lax.scan(step, (zeros_total, zeros_total), inputs)  106 us
    dynamic_update_slice x64, other arithmetic, accumulate(): lax.dynamic_update_slice_in_dim(total, current + summed, glob_at[slot], 0)  94.5 us
    while x160, local copies, waits for them, and re-layouts  91 us
    all_to_all x1, waiting for transfers between devices, body(): lax.all_to_all(key_total.reshape(per_device, tokens * devices, 1, HEAD),...  71.4 us
    all_to_all x1, waiting for transfers between devices, body(): lax.all_to_all(value_total.reshape(per_device, tokens * devices, 1, HEAD)...  50.7 us
    all_to_all x1, waiting for transfers between devices, body(): lax.all_to_all(spread(widen(keys[0])), 'seq', split_axis=2, concat_axis=1...  47.3 us
    dynamic_slice x48, local copies, waits for them, and re-layouts, backward_tiles(): totals, outputs = lax.scan(step, (zeros_total, zeros_total), inputs)  42.2 us
  transfers between devices with their start and end apart: 10, of which 7 were waited for; matrix products, arithmetic and copies ran while one was open for 14% of the time, Pallas kernels for 0%

commit v1 on v0

v1 whole, which is shorter than its diff:
```python
import functools

import jax
import jax.numpy as jnp
from jax import lax
from jax.experimental import pallas as pl
from jax.experimental.pallas import tpu as pltpu
from jax.sharding import PartitionSpec as P

HEADS = 32
KV_HEADS = 4
HEAD = 128
BLOCK = 128
GROUP = HEADS // KV_HEADS
SCALE = HEAD ** -0.5
LOG2E = 1.4426950408889634

NT = (((1,), (1,)), ((), ()))
NN = (((1,), (0,)), ((), ()))


def attend(nblk, nloc, nglob, nrand, first_ref, glob_ref, rand_ref, q_ref, g_ref, k_ref, v_ref, dq_ref, dkv_ref, dk_acc, dv_acc, kt_ref):
    group = pl.program_id(0)
    first = first_ref[0]
    dk_acc[...] = jnp.zeros_like(dk_acc)
    dv_acc[...] = jnp.zeros_like(dv_acc)
    for b in range(nblk):
        rows = slice(b * BLOCK, (b + 1) * BLOCK)
        kt_ref[:, rows] = k_ref[rows, :].T

    def head(j, carry):
        h = group * GROUP + j
        cols = pl.ds(pl.multiple_of(j * HEAD, HEAD), HEAD)
        for b in range(nloc):
            at = first + b
            picks = [lax.rem(at + nblk - 1, nblk), at, lax.rem(at + 1, nblk)]
            picks += [glob_ref[h * nglob + n] for n in range(nglob)]
            picks += [rand_ref[(h * nblk + at) * nrand + n] for n in range(nrand)]
            spans = [pl.ds(pl.multiple_of(p * BLOCK, BLOCK), BLOCK) for p in picks]
            q = q_ref[b * BLOCK : (b + 1) * BLOCK, cols]
            g = g_ref[b * BLOCK : (b + 1) * BLOCK, cols]
            keys = jnp.concatenate([k_ref[s, :] for s in spans], axis=0)
            vals = jnp.concatenate([v_ref[s, :] for s in spans], axis=0)
            s = lax.dot_general(keys, q, NT, preferred_element_type=jnp.float32)
            top = jnp.max(s, axis=0, keepdims=True)
            p = jnp.exp2((s - top) * (SCALE * LOG2E))
            w = p * (1.0 / jnp.sum(p, axis=0, keepdims=True))
            low = w.astype(jnp.bfloat16)
            gw = lax.dot_general(vals, g, NT, preferred_element_type=jnp.float32)
            dot = jnp.sum(low.astype(jnp.float32) * gw, axis=0, keepdims=True)
            ds = (w * (gw - dot) * SCALE).astype(jnp.bfloat16)
            dk = lax.dot_general(ds, q, NN, preferred_element_type=jnp.float32)
            dv = lax.dot_general(low, g, NN, preferred_element_type=jnp.float32)
            kt = jnp.concatenate([kt_ref[:, s] for s in spans], axis=1)
            dqt = lax.dot_general(kt, ds, NN, preferred_element_type=jnp.float32)
            dq_ref[b * BLOCK : (b + 1) * BLOCK, cols] = dqt.T.astype(jnp.bfloat16)
            for n, span in enumerate(spans):
                dk_acc[span, :] += dk[n * BLOCK : (n + 1) * BLOCK, :]
                dv_acc[span, :] += dv[n * BLOCK : (n + 1) * BLOCK, :]
        return carry

    lax.fori_loop(0, GROUP, head, 0)
    dkv_ref[:, :HEAD] = dk_acc[...].astype(jnp.bfloat16)
    dkv_ref[:, HEAD:] = dv_acc[...].astype(jnp.bfloat16)


def local_backward(query, grad, kv, first, global_rows, random_rows):
    tokens = query.shape[0]
    seq = kv.shape[0]
    nblk = seq // BLOCK
    wide = GROUP * HEAD
    kernel = functools.partial(attend, nblk, tokens // BLOCK, global_rows.shape[-1], random_rows.shape[-1])
    smem = pl.BlockSpec(memory_space=pltpu.SMEM)
    return pl.pallas_call(
        kernel,
        grid=(KV_HEADS,),
        in_specs=[
            smem,
            smem,
            smem,
            pl.BlockSpec((tokens, wide), lambda g: (0, g)),
            pl.BlockSpec((tokens, wide), lambda g: (0, g)),
            pl.BlockSpec((seq, HEAD), lambda g: (0, g)),
            pl.BlockSpec((seq, HEAD), lambda g: (0, KV_HEADS + g)),
        ],
        out_specs=[
            pl.BlockSpec((tokens, wide), lambda g: (0, g)),
            pl.BlockSpec((seq, 2 * HEAD), lambda g: (0, g)),
        ],
        out_shape=[
            jax.ShapeDtypeStruct((tokens, HEADS * HEAD), jnp.bfloat16),
            jax.ShapeDtypeStruct((seq, 2 * KV_HEADS * HEAD), jnp.bfloat16),
        ],
        scratch_shapes=[
            pltpu.VMEM((seq, HEAD), jnp.float32),
            pltpu.VMEM((seq, HEAD), jnp.float32),
            pltpu.VMEM((HEAD, seq), jnp.bfloat16),
        ],
        compiler_params=pltpu.CompilerParams(vmem_limit_bytes=56 * 1024 * 1024),
        name="attend",
    )(first.reshape(1), global_rows.reshape(-1), random_rows.reshape(-1), query, grad, kv, kv)


def from_behind(value, axis):
    size = lax.axis_size(axis)
    return lax.ppermute(value, axis, [(i, i - 1) for i in range(1, size)])


def body(queries, keys, values, out_grad, global_blocks, random_blocks):
    tokens = queries.shape[1]
    device = lax.axis_index("seq")
    kv = jnp.concatenate([keys[0], values[0]], axis=1)
    kv = lax.all_gather(kv, "seq", axis=0, tiled=True)
    first = (device * (tokens // BLOCK)).astype(jnp.int32)
    query_grad, partial = local_backward(queries[0], out_grad[0], kv, first, global_blocks[0], random_blocks[0])
    incoming_query = from_behind(query_grad, "pipe")
    mine = lax.psum_scatter(partial, "seq", scatter_dimension=0, tiled=True)
    mine = mine.reshape(tokens, KV_HEADS, 2, HEAD)
    key_grad = mine[:, :, 0].reshape(tokens, KV_HEADS * HEAD)
    value_grad = mine[:, :, 1].reshape(tokens, KV_HEADS * HEAD)
    incoming_key, incoming_value = from_behind((key_grad, value_grad), "pipe")
    return tuple(x[None] for x in (query_grad, key_grad, value_grad, incoming_query, incoming_key, incoming_value))


def solution(mesh):
    part = P("pipe", "seq", None)
    in_specs = (part, part, part, part, P("pipe", None, None), P("pipe", None, None, None))
    return jax.shard_map(body, mesh=mesh, in_specs=in_specs, out_specs=(part,) * 6, check_vma=False)
```

time: 1200 us -> 265 us (0.22); the launches traced: 1180 us -> 264 us
  local copies, waits for them, and re-layouts: 307 us -> 12.4 us
  other arithmetic: 286 us -> 1.88 us
  matrix products: 158 us -> 0 us
  waiting for transfers between devices: 270 us -> 160 us
  loops' own time: 106 us -> 0 us
  Pallas kernels: 0 us -> 67.7 us
  starting transfers between devices: 46.8 us -> 8.29 us
  between operations: 1.44 us -> 14.1 us
    all_to_all x7 -> x0, waiting for transfers between devices: 270 us -> none  [the longest x1 71.4 us: body(): lax.all_to_all(key_total.reshape(per_device, tokens * devices, 1, HEAD),...]
    dynamic_update_slice x160 -> x0, other arithmetic: 255 us -> none  [the longest x80 138 us: accumulate(): lax.dynamic_update_slice_in_dim(total, current + terms[:, offset], start...]
    dot_general x86 -> x0, matrix products: 130 us -> none  [the longest x16 25.2 us: step(): jnp.einsum('gqk,gqd->gkd', weights_low, grad_group, preferred_element_typ...]
    another operation x1 -> x0, loops' own time: 106 us -> none  [backward_tiles(): totals, outputs = lax.scan(step, (zeros_total, zeros_total), inputs)]
    while x160 -> x0, local copies, waits for them, and re-layouts: 91 us -> none
    reduce_scatter x0 -> x1, waiting for transfers between devices: none -> 83.9 us  [body(): mine = lax.psum_scatter(partial, 'seq', scatter_dimension=0, tiled=True)]
    all_gather x0 -> x1, waiting for transfers between devices: none -> 72.7 us  [body(): kv = lax.all_gather(kv, 'seq', axis=0, tiled=True)]
    pallas_call x0 -> x1, Pallas kernels: none -> 67.7 us  [local_backward(): pl.pallas_call(kernel, grid=(KV_HEADS,), in_specs=[smem, smem, smem, pl.B...]
  transfers between devices with their start and end apart: 10 -> 5, of which waited for: 7 -> 4; matrix products, arithmetic and copies ran while one was open for 14% -> 4% of each run, Pallas kernels for 0% -> 0%
where the time goes in v1:
time: 265 us; the launch traced here: 264 us
  waiting for transfers between devices  160 us (60%)
  Pallas kernels  67.7 us (26%)
  between operations  14.1 us (5%)
  local copies, waits for them, and re-layouts  12.4 us (5%)
  starting transfers between devices  8.29 us (3%)
    reduce_scatter x1, waiting for transfers between devices, body(): mine = lax.psum_scatter(partial, 'seq', scatter_dimension=0, tiled=True)  83.9 us
    all_gather x1, waiting for transfers between devices, body(): kv = lax.all_gather(kv, 'seq', axis=0, tiled=True)  72.7 us
    pallas_call x1, Pallas kernels, local_backward(): pl.pallas_call(kernel, grid=(KV_HEADS,), in_specs=[smem, smem, smem, pl.B...  67.7 us
    ppermute x3, starting transfers between devices, from_behind(): return lax.ppermute(value, axis, [(i, i - 1) for i in range(1, size)])  8.21 us
    unnamed x9, local copies, waits for them, and re-layouts  8.09 us
  transfers between devices with their start and end apart: 5, of which 4 were waited for; matrix products, arithmetic and copies ran while one was open for 4% of the time, Pallas kernels for 0%

profile of v1, /device:TPU:1, one launch (start us, length us, event | category | flops | bytes accessed | tf_op | source)
XLA Modules:
  0.0 264.3 jit_solution(3212477084278479526)
XLA Ops:
  7.2 0.0 all-gather.2.cloned.1.call-start
  7.2 1.9 pad_maximum_fusion
  9.1 0.0 reduce-scatter.2.cloned.1.call-start
  9.2 0.8 copy.13
  9.9 0.6 reshape_squeeze.12.glob_ref
  10.5 0.9 copy.14
  11.5 0.8 reshape_squeeze.13.rand_ref
  12.3 72.7 %all-gather.2.cloned.1.call-done.k_ref.v_ref = bf16[2048,1024]{1,0:T(8,128)(2,1)} async-done(((bf16[256,1024]{1,0:T(8,128)(2,1)}), bf16[2048,1024]{1,0:T(8,128)(2,1)}) %all-gather.2.cloned.1.call-update) | async-done | bytes 4194320 | tf_op jit(solution)/shard_map/all_gather | solution.py:113
  85.0 67.7 %attend.1 = (bf16[256,4096]{1,0:T(8,128)(2,1)}, bf16[2048,1024]{1,0:T(8,128)(2,1)}) custom-call(s32[1]{0:T(128)} %bitcast.first_ref, s32[64]{0:T(128)} %reshape_squeeze.12.glob_ref, s32[1536]{0:T(1024)} %reshape_squeeze.13.rand_ref, bf16[256,4096]{1,0:T(8,128)(2,1)} %bitcast.16, bf16[256,4096]{1,0:T(8,128)(2,1)} %bitcast.17, ...), custom_call_target="tpu_custom_call" | custom-call | tf_op jit(solution)/shard_map/attend/pallas_call | solution.py:74
  152.7 3.8 %collective-permute-start = (bf16[256,4096]{1,0:T(8,128)(2,1)}, bf16[256,4096]{1,0:T(8,128)(2,1)S(1)}, u32[]{:S(2)}, u32[]{:S(2)}) collective-permute-start(bf16[256,4096]{1,0:T(8,128)(2,1)} %get-tuple-element.8), channel_id=1, source_target_pairs={{8,0},{16,8},{24,16},{9,1},{17,9},{25,17},{10,2},{18,10},{26,18},{... | collective-permute-start | bytes 6291464 | tf_op jit(solution)/shard_map/ppermute | solution.py:106
  156.5 83.9 %reduce-scatter.2.cloned.1.call-done = bf16[256,1024]{1,0:T(8,128)(2,1)} async-done(((bf16[2048,1024]{1,0:T(8,128)(2,1)}), bf16[256,1024]{1,0:T(8,128)(2,1)}) %reduce-scatter.2.cloned.1.call-update) | async-done | bytes 524304 | tf_op jit(solution)/shard_map/reduce_scatter | solution.py:117
  240.4 1.4 reshape.19
  241.8 1.5 fusion
  243.3 1.2 copy.21
  244.6 2.5 collective-permute-start.1
  247.1 0.5 copy.22
  247.6 1.9 collective-permute-start.2
  249.5 0.8 copy.17
  250.4 0.8 copy.18
  251.2 1.0 collective-permute-done.1
  252.3 0.8 copy.19
  253.1 2.2 collective-permute-done.2
  255.3 0.8 copy.20
  256.1 1.3 copy.24
  (3 shorter events, 0.0 us)
Async XLA Ops:
  7.2 77.9 %all-gather.2.cloned.1.call-start = ((), (), s32[]{:S(2)}) async-start(), calls=%async_computation.1 | async-start | bytes 4718592 | tf_op jit(solution)/shard_map/all_gather | solution.py:113
  9.1 231.3 %reduce-scatter.2.cloned.1.call-start = ((), (), s32[]{:S(2)}) async-start(), calls=%async_computation.2 | async-start | bytes 4718592 | tf_op jit(solution)/shard_map/reduce_scatter | solution.py:117
  152.7 96.8 %collective-permute-start = (bf16[256,4096]{1,0:T(8,128)(2,1)}, bf16[256,4096]{1,0:T(8,128)(2,1)S(1)}, u32[]{:S(2)}, u32[]{:S(2)}) collective-permute-start(bf16[256,4096]{1,0:T(8,128)(2,1)} %get-tuple-element.8), channel_id=1, source_target_pairs={{8,0},{16,8},{24,16},{9,1},{17,9},{25,17},{10,2},{18,10},{26,18},{... | collective-permute-start | bytes 6291464 | tf_op jit(solution)/shard_map/ppermute | solution.py:106
  244.6 7.7 %collective-permute-start.1 = (bf16[256,512]{0,1:T(8,128)(2,1)S(1)}, bf16[256,512]{0,1:T(8,128)(2,1)S(1)}, u32[]{:S(2)}, u32[]{:S(2)}) collective-permute-start(bf16[256,512]{0,1:T(8,128)(2,1)S(1)} %bitcast.18), channel_id=1, source_target_pairs={{8,0},{16,8},{24,16},{9,1},{17,9},{25,17},{10,2},{18,10},{26,18},{... | collective-permute-start | bytes 786440 | tf_op jit(solution)/shard_map/ppermute | solution.py:106
  247.6 7.7 %collective-permute-start.2 = (bf16[256,512]{0,1:T(8,128)(2,1)S(1)}, bf16[256,512]{0,1:T(8,128)(2,1)S(1)}, u32[]{:S(2)}, u32[]{:S(2)}) collective-permute-start(bf16[256,512]{0,1:T(8,128)(2,1)S(1)} %bitcast.20), channel_id=1, source_target_pairs={{8,0},{16,8},{24,16},{9,1},{17,9},{25,17},{10,2},{18,10},{26,18},{... | collective-permute-start | bytes 786440 | tf_op jit(solution)/shard_map/ppermute | solution.py:106
Sparse Core Ops, SparseCore 0:
  10.7 74.2 all-gather.1
  152.8 87.5 reduce-scatter.1

commit v2 on v1

--- a/solution.py
+++ b/solution.py
@@ -64,9 +64,9 @@
     dkv_ref[:, HEAD:] = dv_acc[...].astype(jnp.bfloat16)
 
 
-def local_backward(query, grad, kv, first, global_rows, random_rows):
+def local_backward(query, grad, k_all, v_all, first, global_rows, random_rows):
     tokens = query.shape[0]
-    seq = kv.shape[0]
+    seq = k_all.shape[0]
     nblk = seq // BLOCK
     wide = GROUP * HEAD
     kernel = functools.partial(attend, nblk, tokens // BLOCK, global_rows.shape[-1], random_rows.shape[-1])
@@ -81,7 +81,7 @@
             pl.BlockSpec((tokens, wide), lambda g: (0, g)),
             pl.BlockSpec((tokens, wide), lambda g: (0, g)),
             pl.BlockSpec((seq, HEAD), lambda g: (0, g)),
-            pl.BlockSpec((seq, HEAD), lambda g: (0, KV_HEADS + g)),
+            pl.BlockSpec((seq, HEAD), lambda g: (0, g)),
         ],
         out_specs=[
             pl.BlockSpec((tokens, wide), lambda g: (0, g)),
@@ -98,7 +98,273 @@
         ],
         compiler_params=pltpu.CompilerParams(vmem_limit_bytes=56 * 1024 * 1024),
         name="attend",
-    )(first.reshape(1), global_rows.reshape(-1), random_rows.reshape(-1), query, grad, kv, kv)
+    )(first.reshape(1), global_rows.reshape(-1), random_rows.reshape(-1), query, grad, k_all, v_all)
+
+
+def ring_place():
+    me = lax.axis_index("seq")
+    z = me // 2
+    x = me % 2
+    return me, z, x
+
+
+def greet(edges):
+    barrier = pltpu.get_barrier_semaphore()
+    for there, to in edges:
+        @pl.when(there)
+        def _(to=to):
+            pl.semaphore_signal(barrier, inc=1, device_id=to, device_id_type=pl.DeviceIdType.MESH)
+    pl.semaphore_wait(barrier, sum(jnp.where(there, 1, 0) for there, _ in edges))
+
+
+def gather_kernel(n, k_ref, v_ref, ko_ref, vo_ref, own_sem, send_sem, recv_sem):
+    levels = n // 2
+    me, z, x = ring_place()
+    partner, up, down = me + 1 - 2 * x, me + 2, me - 2
+    tokens = k_ref.shape[0]
+    sources, outs = (k_ref, v_ref), (ko_ref, vo_ref)
+    greet([(z >= 0, {"seq": partner}), (z < levels - 1, {"seq": up}), (z > 0, {"seq": down})])
+
+    def place(i, shard):
+        return outs[i].at[pl.ds(pl.multiple_of(shard * tokens, tokens), tokens), :]
+
+    def copy(i, shard, way, to, src=None):
+        spot = place(i, shard)
+        return pltpu.make_async_remote_copy(
+            src_ref=spot if src is None else src,
+            dst_ref=spot,
+            send_sem=send_sem.at[way, i, shard],
+            recv_sem=recv_sem.at[i, shard],
+            device_id={"seq": to},
+            device_id_type=pl.DeviceIdType.MESH,
+        )
+
+    owns = [pltpu.make_async_copy(sources[i], place(i, me), own_sem.at[i]) for i in range(2)]
+    for i in range(2):
+        @pl.when(z < levels - 1)
+        def _(i=i):
+            copy(i, me, 0, up, sources[i]).start()
+
+        @pl.when(z > 0)
+        def _(i=i):
+            copy(i, me, 1, down, sources[i]).start()
+
+        copy(i, me, 2, partner, sources[i]).start()
+    for own in owns:
+        own.start()
+    for t in range(1, levels):
+        for i in range(2):
+            @pl.when(z >= t)
+            def _(i=i, t=t):
+                shard = me - 2 * t
+                copy(i, shard, 2, partner).wait_recv()
+
+                @pl.when(z < levels - 1)
+                def _():
+                    copy(i, shard, 0, up).start()
+
+                copy(i, shard, 2, partner).start()
+
+            @pl.when(z + t < levels)
+            def _(i=i, t=t):
+                shard = me + 2 * t
+                copy(i, shard, 2, partner).wait_recv()
+
+                @pl.when(z > 0)
+                def _():
+                    copy(i, shard, 1, down).start()
+
+                copy(i, shard, 2, partner).start()
+    for i in range(2):
+        for level in range(levels):
+            copy(i, 2 * level + 1 - x, 2, partner).wait_recv()
+            copy(i, 2 * level + x, 2, partner).wait_send()
+
+            @pl.when((level <= z) & (z < levels - 1))
+            def _(i=i, level=level):
+                copy(i, 2 * level + x, 0, up).wait_send()
+
+            @pl.when((level >= z) & (z > 0))
+            def _(i=i, level=level):
+                copy(i, 2 * level + x, 1, down).wait_send()
+    for own in owns:
+        own.wait()
+
+
+def gather_rows(keys, values):
+    n = lax.axis_size("seq")
+    tokens, width = keys.shape
+    whole = jax.ShapeDtypeStruct((n * tokens, width), keys.dtype)
+    hbm = pl.BlockSpec(memory_space=pl.ANY)
+    return pl.pallas_call(
+        functools.partial(gather_kernel, n),
+        in_specs=[hbm, hbm],
+        out_specs=[hbm, hbm],
+        out_shape=[whole, whole],
+        scratch_shapes=[
+            pltpu.SemaphoreType.DMA((2,)),
+            pltpu.SemaphoreType.DMA((3, 2, n)),
+            pltpu.SemaphoreType.DMA((2, n)),
+        ],
+        compiler_params=pltpu.CompilerParams(collective_id=0, has_side_effects=True),
+        name="gather_rows",
+    )(keys, values)
+
+
+PIECES = 2
+
+
+def reduce_kernel(n, sections, part_ref, dk_ref, dv_ref, ik_ref, iv_ref, xbuf, ubuf, dbuf, xs, xr, us, ur, ds, dr, ps, pr):
+    levels = n // 2
+    me, z, x = ring_place()
+    section = lax.axis_index("pipe")
+    partner, up, down = me + 1 - 2 * x, me + 2, me - 2
+    tokens = dk_ref.shape[0]
+    rows = tokens // PIECES
+    greet([
+        (z >= 0, {"seq": partner}),
+        (z < levels - 1, {"seq": up}),
+        (z > 0, {"seq": down}),
+        (section > 0, {"pipe": section - 1}),
+        (section < sections - 1, {"pipe": section + 1}),
+    ])
+
+    def at(ref, level, k):
+        return ref.at[pl.ds(pl.multiple_of(level * tokens + k * rows, rows), rows), :]
+
+    def remote(src, dst, send, recv, to):
+        return pltpu.make_async_remote_copy(
+            src_ref=src, dst_ref=dst, send_sem=send, recv_sem=recv,
+            device_id=to, device_id_type=pl.DeviceIdType.MESH,
+        )
+
+    def across(level, k):
+        return remote(at(part_ref, 2 * level + 1 - x, k), at(xbuf, level, k), xs.at[level, k], xr.at[level, k], {"seq": partner})
+
+    def upward(level, k):
+        return remote(at(xbuf, level, k), at(ubuf, level, k), us.at[level, k], ur.at[level, k], {"seq": up})
+
+    def downward(level, k):
+        return remote(at(xbuf, level, k), at(dbuf, level, k), ds.at[level, k], dr.at[level, k], {"seq": down})
+
+    def each_far(action):
+        for t in range(levels - 1, 0, -1):
+            for k in range(PIECES):
+                @pl.when(z + t < levels)
+                def _(t=t, k=k):
+                    action(z + t, k, True)
+
+                @pl.when(z >= t)
+                def _(t=t, k=k):
+                    action(z - t, k, False)
+
+    each_far(lambda level, k, rising: across(level, k).start())
+    for k in range(PIECES):
+        across(z, k).start()
+
+    def load(ref, level, k):
+        return ref[pl.ds(pl.multiple_of(level * tokens + k * rows, rows), rows), :]
+
+    def add(level, k, value):
+        spot = pl.ds(pl.multiple_of(level * tokens + k * rows, rows), rows)
+        xbuf[spot, :] = (xbuf[spot, :].astype(jnp.float32) + value.astype(jnp.float32)).astype(jnp.bfloat16)
+
+    def pass_on(level, k, rising):
+        across(level, k).wait_recv()
+        mine = load(part_ref, 2 * level + x, k).astype(jnp.float32)
+        if rising:
+            @pl.when(z > 0)
+            def _():
+                upward(level, k).wait_recv()
+                add(level, k, mine + load(ubuf, level, k).astype(jnp.float32))
+
+            @pl.when(z == 0)
+            def _():
+                add(level, k, mine)
+
+            upward(level, k).start()
+        else:
+            @pl.when(z < levels - 1)
+            def _():
+                downward(level, k).wait_recv()
+                add(level, k, mine + load(dbuf, level, k).astype(jnp.float32))
+
+            @pl.when(z == levels - 1)
+            def _():
+                add(level, k, mine)
+
+            downward(level, k).start()
+
+    each_far(pass_on)
+
+    def shift(src, dst, i, k):
+        spot = pl.ds(k * rows, rows)
+        return remote(src.at[spot, :], dst.at[spot, :], ps.at[i, k], pr.at[i, k], {"pipe": section - 1})
+
+    pairs = ((dk_ref, ik_ref), (dv_ref, iv_ref))
+    for k in range(PIECES):
+        across(z, k).wait_recv()
+
+        @pl.when(z > 0)
+        def _(k=k):
+            upward(z, k).wait_recv()
+
+        @pl.when(z < levels - 1)
+        def _(k=k):
+            downward(z, k).wait_recv()
+
+        below = jnp.where(z > 0, load(ubuf, z, k).astype(jnp.float32), 0.0)
+        above = jnp.where(z < levels - 1, load(dbuf, z, k).astype(jnp.float32), 0.0)
+        total = load(part_ref, me, k).astype(jnp.float32) + load(xbuf, z, k).astype(jnp.float32)
+        total = (total + below + above).astype(jnp.bfloat16)
+        spot = slice(k * rows, (k + 1) * rows)
+        for g in range(KV_HEADS):
+            cols = slice(g * HEAD, (g + 1) * HEAD)
+            dk_ref[spot, cols] = total[:, 2 * g * HEAD : (2 * g + 1) * HEAD]
+            dv_ref[spot, cols] = total[:, (2 * g + 1) * HEAD : (2 * g + 2) * HEAD]
+
+        @pl.when(section > 0)
+        def _(k=k):
+            for i, (src, dst) in enumerate(pairs):
+                shift(src, dst, i, k).start()
+
+    @pl.when(section == sections - 1)
+    def _():
+        ik_ref[...] = jnp.zeros_like(ik_ref)
+        iv_ref[...] = jnp.zeros_like(iv_ref)
+
+    each_far(lambda level, k, rising: (across(level, k).wait_send(), (upward if rising else downward)(level, k).wait_send()))
+    for k in range(PIECES):
+        across(z, k).wait_send()
+        for i, (src, dst) in enumerate(pairs):
+            @pl.when(section < sections - 1)
+            def _(i=i, k=k, src=src, dst=dst):
+                shift(src, dst, i, k).wait_recv()
+
+            @pl.when(section > 0)
+            def _(i=i, k=k, src=src, dst=dst):
+                shift(src, dst, i, k).wait_send()
+
+
+def reduce_rows(partial):
+    n = lax.axis_size("seq")
+    tokens = partial.shape[0] // n
+    wide = partial.shape[1]
+    half = jax.ShapeDtypeStruct((tokens, wide // 2), partial.dtype)
+    vmem = pl.BlockSpec(memory_space=pltpu.VMEM)
+    slots = pltpu.VMEM((n // 2 * tokens, wide), partial.dtype)
+    dma = pltpu.SemaphoreType.DMA((n // 2, PIECES))
+    return pl.pallas_call(
+        functools.partial(reduce_kernel, n, lax.axis_size("pipe")),
+        in_specs=[vmem],
+        out_specs=[vmem] * 4,
+        out_shape=[half] * 4,
+        scratch_shapes=[slots] * 3 + [dma] * 6 + [pltpu.SemaphoreType.DMA((2, PIECES))] * 2,
+        compiler_params=pltpu.CompilerParams(
+            collective_id=1, has_side_effects=True, vmem_limit_bytes=58 * 1024 * 1024
+        ),
+        name="reduce_rows",
+    )(partial)
 
 
 def from_behind(value, axis):
@@ -109,16 +375,11 @@
 def body(queries, keys, values, out_grad, global_blocks, random_blocks):
     tokens = queries.shape[1]
     device = lax.axis_index("seq")
-    kv = jnp.concatenate([keys[0], values[0]], axis=1)
-    kv = lax.all_gather(kv, "seq", axis=0, tiled=True)
+    k_all, v_all = gather_rows(keys[0], values[0])
     first = (device * (tokens // BLOCK)).astype(jnp.int32)
-    query_grad, partial = local_backward(queries[0], out_grad[0], kv, first, global_blocks[0], random_blocks[0])
+    query_grad, partial = local_backward(queries[0], out_grad[0], k_all, v_all, first, global_blocks[0], random_blocks[0])
     incoming_query = from_behind(query_grad, "pipe")
-    mine = lax.psum_scatter(partial, "seq", scatter_dimension=0, tiled=True)
-    mine = mine.reshape(tokens, KV_HEADS, 2, HEAD)
-    key_grad = mine[:, :, 0].reshape(tokens, KV_HEADS * HEAD)
-    value_grad = mine[:, :, 1].reshape(tokens, KV_HEADS * HEAD)
-    incoming_key, incoming_value = from_behind((key_grad, value_grad), "pipe")
+    key_grad, value_grad, incoming_key, incoming_value = reduce_rows(partial)
     return tuple(x[None] for x in (query_grad, key_grad, value_grad, incoming_query, incoming_key, incoming_value))
 
 

time: 265 us -> 188 us (0.71)
  waiting for transfers between devices: 160 us -> 0.01 us
  Pallas kernels: 67.7 us -> 174 us
  between operations: 14.1 us -> 0.68 us
  starting transfers between devices: 8.29 us -> 3.45 us
  local copies, waits for them, and re-layouts: 12.4 us -> 9.19 us
    pallas_call x0 -> x2, Pallas kernels: none -> 107 us  [the longest x1 57.3 us: reduce_rows(): pl.pallas_call(functools.partial(reduce_kernel, n, lax.axis_size('pipe'))...]
    reduce_scatter x1 -> x0, waiting for transfers between devices: 83.9 us -> none  [body(): mine = lax.psum_scatter(partial, 'seq', scatter_dimension=0, tiled=True)]
    all_gather x1 -> x0, waiting for transfers between devices: 72.7 us -> none  [body(): kv = lax.all_gather(kv, 'seq', axis=0, tiled=True)]
    ppermute x3 -> x1, starting transfers between devices: 8.21 us -> 3.45 us  [from_behind(): return lax.ppermute(value, axis, [(i, i - 1) for i in range(1, size)])]
    ppermute x3 -> x1, waiting for transfers between devices: 3.22 us -> 0.01 us  [from_behind(): return lax.ppermute(value, axis, [(i, i - 1) for i in range(1, size)])]
    unnamed x9 -> x11, local copies, waits for them, and re-layouts: 8.09 us -> 7.76 us
  transfers between devices with their start and end apart: 5 -> 1, of which waited for: 4 -> 0; matrix products, arithmetic and copies ran while one was open for 4% -> 0% of each run, Pallas kernels for 0% -> 31%
where the time goes in v2:
time: 188 us
  Pallas kernels  174 us (93%)
  local copies, waits for them, and re-layouts  9.19 us (5%)
  starting transfers between devices  3.45 us (2%)
    pallas_call x1, Pallas kernels, local_backward(): pl.pallas_call(kernel, grid=(KV_HEADS,), in_specs=[smem, smem, smem, pl.B...  67.6 us
    pallas_call x1, Pallas kernels, reduce_rows(): pl.pallas_call(functools.partial(reduce_kernel, n, lax.axis_size('pipe'))...  57.3 us
    pallas_call x1, Pallas kernels, gather_rows(): pl.pallas_call(functools.partial(gather_kernel, n), in_specs=[hbm, hbm],...  49.3 us
    unnamed x11, local copies, waits for them, and re-layouts  7.76 us
  transfers between devices with their start and end apart: 1, of which 0 were waited for; matrix products, arithmetic and copies ran while one was open for 0% of the time, Pallas kernels for 31%

profile of v2, /device:TPU:1, one launch (start us, length us, event | category | flops | bytes accessed | tf_op | source)
XLA Modules:
  0.0 187.6 jit_solution(12843421402973748824)
XLA Ops:
  0.6 0.8 copy.13
  1.4 0.6 reshape_squeeze.6.glob_ref
  2.0 0.9 copy.14
  3.0 0.8 reshape_squeeze.7.rand_ref
  3.8 49.3 %gather_rows.1 = (bf16[2048,512]{1,0:T(8,128)(2,1)}, bf16[2048,512]{1,0:T(8,128)(2,1)}) custom-call(bf16[256,512]{1,0:T(8,128)(2,1)} %bitcast.16, bf16[256,512]{1,0:T(8,128)(2,1)} %bitcast.17), custom_call_target="tpu_custom_call" | custom-call | tf_op jit(solution)/shard_map/gather_rows/pallas_call | solution.py:199
  53.1 67.6 %attend.1 = (bf16[256,4096]{1,0:T(8,128)(2,1)}, bf16[2048,1024]{1,0:T(8,128)(2,1)}) custom-call(s32[1]{0:T(128)} %bitcast.first_ref, s32[64]{0:T(128)} %reshape_squeeze.6.glob_ref, s32[1536]{0:T(1024)} %reshape_squeeze.7.rand_ref, bf16[256,4096]{1,0:T(8,128)(2,1)} %bitcast.13, bf16[256,4096]{1,0:T(8,128)(2,1)} %bitcast.14, ...), custom_call_target="tpu_custom_call" | custom-call | tf_op jit(solution)/shard_map/attend/pallas_call | solution.py:74
  120.7 3.5 %collective-permute-start = (bf16[256,4096]{1,0:T(8,128)(2,1)}, bf16[256,4096]{1,0:T(8,128)(2,1)S(1)}, u32[]{:S(2)}, u32[]{:S(2)}) collective-permute-start(bf16[256,4096]{1,0:T(8,128)(2,1)} %get-tuple-element.16), channel_id=1, source_target_pairs={{8,0},{16,8},{24,16},{9,1},{17,9},{25,17},{10,2},{18,10},{26,18},{... | collective-permute-start | bytes 6291464 | tf_op jit(solution)/shard_map/ppermute | solution.py:372
  124.2 57.3 %reduce_rows.1 = (bf16[256,512]{1,0:T(8,128)(2,1)}, bf16[256,512]{1,0:T(8,128)(2,1)}, bf16[256,512]{1,0:T(8,128)(2,1)}, bf16[256,512]{1,0:T(8,128)(2,1)}) custom-call(bf16[2048,1024]{1,0:T(8,128)(2,1)} %get-tuple-element.17.part_ref), custom_call_target="tpu_custom_call" | custom-call | tf_op jit(solution)/shard_map/reduce_rows/pallas_call | solution.py:357
  181.5 0.0 collective-permute-done
  181.5 1.7 copy.20
  183.2 1.7 copy.21
  184.9 0.0 copy-start.1
  184.9 0.0 copy-start
  184.9 1.3 copy.22
  186.2 0.0 copy-done.1
  186.2 0.7 copy.23
  186.9 0.0 copy-done
  186.9 0.7 copy.24
Async XLA Ops:
  120.7 60.8 %collective-permute-start = (bf16[256,4096]{1,0:T(8,128)(2,1)}, bf16[256,4096]{1,0:T(8,128)(2,1)S(1)}, u32[]{:S(2)}, u32[]{:S(2)}) collective-permute-start(bf16[256,4096]{1,0:T(8,128)(2,1)} %get-tuple-element.16), channel_id=1, source_target_pairs={{8,0},{16,8},{24,16},{9,1},{17,9},{25,17},{10,2},{18,10},{26,18},{... | collective-permute-start | bytes 6291464 | tf_op jit(solution)/shard_map/ppermute | solution.py:372
  184.9 1.3 copy-start.1
  184.9 2.0 %copy-start = (bf16[256,512]{1,0:T(8,128)(2,1)S(1)}, bf16[256,512]{1,0:T(8,128)(2,1)}, u32[]{:S(2)}) copy-start(bf16[256,512]{1,0:T(8,128)(2,1)} %get-tuple-element.21) | copy-start | bytes 786436

commit v3 on v2

--- a/solution.py
+++ b/solution.py
@@ -28,38 +28,58 @@
         rows = slice(b * BLOCK, (b + 1) * BLOCK)
         kt_ref[:, rows] = k_ref[rows, :].T
 
+    def listed(h, b):
+        at = first + b
+        picks = [lax.rem(at + nblk - 1, nblk), at, lax.rem(at + 1, nblk)]
+        picks += [glob_ref[h * nglob + n] for n in range(nglob)]
+        picks += [rand_ref[(h * nblk + at) * nrand + n] for n in range(nrand)]
+        return [pl.ds(pl.multiple_of(p * BLOCK, BLOCK), BLOCK) for p in picks]
+
+    def products(spans, rows, cols):
+        q, g = q_ref[rows, cols], g_ref[rows, cols]
+        keys = jnp.concatenate([k_ref[s, :] for s in spans], axis=0)
+        vals = jnp.concatenate([v_ref[s, :] for s in spans], axis=0)
+        s = lax.dot_general(keys, q, NT, preferred_element_type=jnp.float32)
+        gw = lax.dot_general(vals, g, NT, preferred_element_type=jnp.float32)
+        cut = lambda x: [x[n * BLOCK : (n + 1) * BLOCK, :] for n in range(len(spans))]
+        return cut(s), cut(gw)
+
+    def gradients(spans, rows, cols, s, gw):
+        q, g = q_ref[rows, cols], g_ref[rows, cols]
+        count = len(spans)
+        top = functools.reduce(jnp.maximum, [jnp.max(x, axis=0, keepdims=True) for x in s])
+        p, total, mixed = [], 0.0, 0.0
+        for x, y in zip(s, gw):
+            e = jnp.exp2((x - top) * (SCALE * LOG2E))
+            p.append(e)
+            total = total + jnp.sum(e, axis=0, keepdims=True)
+            mixed = mixed + jnp.sum(e * y, axis=0, keepdims=True)
+        inv = 1.0 / total
+        dot = mixed * inv
+        inv_scaled = inv * SCALE
+        low = jnp.concatenate([(x * inv).astype(jnp.bfloat16) for x in p], axis=0)
+        ds = jnp.concatenate(
+            [((x * inv_scaled) * (y - dot)).astype(jnp.bfloat16) for x, y in zip(p, gw)], axis=0
+        )
+        dv = lax.dot_general(low, g, NN, preferred_element_type=jnp.float32)
+        dk = lax.dot_general(ds, q, NN, preferred_element_type=jnp.float32)
+        kt = jnp.concatenate([kt_ref[:, s] for s in spans], axis=1)
+        dqt = lax.dot_general(kt, ds, NN, preferred_element_type=jnp.float32)
+        dq_ref[rows, cols] = dqt.T.astype(jnp.bfloat16)
+        for n, span in enumerate(spans):
+            dk_acc[span, :] += dk[n * BLOCK : (n + 1) * BLOCK, :]
+            dv_acc[span, :] += dv[n * BLOCK : (n + 1) * BLOCK, :]
+
     def head(j, carry):
         h = group * GROUP + j
         cols = pl.ds(pl.multiple_of(j * HEAD, HEAD), HEAD)
-        for b in range(nloc):
-            at = first + b
-            picks = [lax.rem(at + nblk - 1, nblk), at, lax.rem(at + 1, nblk)]
-            picks += [glob_ref[h * nglob + n] for n in range(nglob)]
-            picks += [rand_ref[(h * nblk + at) * nrand + n] for n in range(nrand)]
-            spans = [pl.ds(pl.multiple_of(p * BLOCK, BLOCK), BLOCK) for p in picks]
-            q = q_ref[b * BLOCK : (b + 1) * BLOCK, cols]
-            g = g_ref[b * BLOCK : (b + 1) * BLOCK, cols]
-            keys = jnp.concatenate([k_ref[s, :] for s in spans], axis=0)
-            vals = jnp.concatenate([v_ref[s, :] for s in spans], axis=0)
-            s = lax.dot_general(keys, q, NT, preferred_element_type=jnp.float32)
-            top = jnp.max(s, axis=0, keepdims=True)
-            p = jnp.exp2((s - top) * (SCALE * LOG2E))
-            w = p * (1.0 / jnp.sum(p, axis=0, keepdims=True))
-            low = w.astype(jnp.bfloat16)
-            gw = lax.dot_general(vals, g, NT, preferred_element_type=jnp.float32)
-            dot = jnp.sum(low.astype(jnp.float32) * gw, axis=0, keepdims=True)
-            ds = (w * (gw - dot) * SCALE).astype(jnp.bfloat16)
-            dk = lax.dot_general(ds, q, NN, preferred_element_type=jnp.float32)
-            dv = lax.dot_general(low, g, NN, preferred_element_type=jnp.float32)
-            kt = jnp.concatenate([kt_ref[:, s] for s in spans], axis=1)
-            dqt = lax.dot_general(kt, ds, NN, preferred_element_type=jnp.float32)
-            dq_ref[b * BLOCK : (b + 1) * BLOCK, cols] = dqt.T.astype(jnp.bfloat16)
-            for n, span in enumerate(spans):
-                dk_acc[span, :] += dk[n * BLOCK : (n + 1) * BLOCK, :]
-                dv_acc[span, :] += dv[n * BLOCK : (n + 1) * BLOCK, :]
+        work = [(listed(h, b), slice(b * BLOCK, (b + 1) * BLOCK), cols) for b in range(nloc)]
+        made = [products(*w) for w in work]
+        for w, m in zip(work, made):
+            gradients(*w, *m)
         return carry
 
-    lax.fori_loop(0, GROUP, head, 0)
+    lax.fori_loop(0, GROUP, head, 0, unroll=2)
     dkv_ref[:, :HEAD] = dk_acc[...].astype(jnp.bfloat16)
     dkv_ref[:, HEAD:] = dv_acc[...].astype(jnp.bfloat16)
 

time: 188 us -> 167 us (0.89)
  Pallas kernels: 174 us -> 153 us
    pallas_call x1, Pallas kernels: 67.6 us -> 46.6 us  [local_backward(): pl.pallas_call(kernel, grid=(KV_HEADS,), in_specs=[smem, smem, smem, pl.B...]
  transfers between devices with their start and end apart: 1 -> 1, of which waited for: 0 -> 0; matrix products, arithmetic and copies ran while one was open for 0% -> 0% of each run, Pallas kernels for 31% -> 34%
where the time goes in v3:
time: 167 us
  Pallas kernels  153 us (92%)
  local copies, waits for them, and re-layouts  9.19 us (6%)
  starting transfers between devices  3.42 us (2%)
    pallas_call x1, Pallas kernels, reduce_rows(): pl.pallas_call(functools.partial(reduce_kernel, n, lax.axis_size('pipe'))...  57.5 us
    pallas_call x1, Pallas kernels, gather_rows(): pl.pallas_call(functools.partial(gather_kernel, n), in_specs=[hbm, hbm],...  49.3 us
    pallas_call x1, Pallas kernels, local_backward(): pl.pallas_call(kernel, grid=(KV_HEADS,), in_specs=[smem, smem, smem, pl.B...  46.6 us
    unnamed x11, local copies, waits for them, and re-layouts  7.76 us
    ppermute x1, starting transfers between devices, from_behind(): return lax.ppermute(value, axis, [(i, i - 1) for i in range(1, size)])  3.42 us
  transfers between devices with their start and end apart: 1, of which 0 were waited for; matrix products, arithmetic and copies ran while one was open for 0% of the time, Pallas kernels for 34%

profile of v3, /device:TPU:1, one launch (start us, length us, event | category | flops | bytes accessed | tf_op | source)
XLA Modules:
  0.0 166.7 jit_solution(922657527271983079)
XLA Ops:
  0.6 0.8 copy.13
  1.4 0.6 reshape_squeeze.6.glob_ref
  2.0 0.9 copy.14
  3.0 0.8 reshape_squeeze.7.rand_ref
  3.8 49.3 %gather_rows.1 = (bf16[2048,512]{1,0:T(8,128)(2,1)}, bf16[2048,512]{1,0:T(8,128)(2,1)}) custom-call(bf16[256,512]{1,0:T(8,128)(2,1)} %bitcast.16, bf16[256,512]{1,0:T(8,128)(2,1)} %bitcast.17), custom_call_target="tpu_custom_call" | custom-call | tf_op jit(solution)/shard_map/gather_rows/pallas_call | solution.py:219
  53.1 46.6 %attend.1 = (bf16[256,4096]{1,0:T(8,128)(2,1)}, bf16[2048,1024]{1,0:T(8,128)(2,1)}) custom-call(s32[1]{0:T(128)} %bitcast.first_ref, s32[64]{0:T(128)} %reshape_squeeze.6.glob_ref, s32[1536]{0:T(1024)} %reshape_squeeze.7.rand_ref, bf16[256,4096]{1,0:T(8,128)(2,1)} %bitcast.13, bf16[256,4096]{1,0:T(8,128)(2,1)} %bitcast.14, ...), custom_call_target="tpu_custom_call" | custom-call | tf_op jit(solution)/shard_map/attend/pallas_call | solution.py:94
  99.7 3.4 %collective-permute-start = (bf16[256,4096]{1,0:T(8,128)(2,1)}, bf16[256,4096]{1,0:T(8,128)(2,1)S(1)}, u32[]{:S(2)}, u32[]{:S(2)}) collective-permute-start(bf16[256,4096]{1,0:T(8,128)(2,1)} %get-tuple-element.16), channel_id=1, source_target_pairs={{8,0},{16,8},{24,16},{9,1},{17,9},{25,17},{10,2},{18,10},{26,18},{... | collective-permute-start | bytes 6291464 | tf_op jit(solution)/shard_map/ppermute | solution.py:392
  103.1 57.5 %reduce_rows.1 = (bf16[256,512]{1,0:T(8,128)(2,1)}, bf16[256,512]{1,0:T(8,128)(2,1)}, bf16[256,512]{1,0:T(8,128)(2,1)}, bf16[256,512]{1,0:T(8,128)(2,1)}) custom-call(bf16[2048,1024]{1,0:T(8,128)(2,1)} %get-tuple-element.17.part_ref), custom_call_target="tpu_custom_call" | custom-call | tf_op jit(solution)/shard_map/reduce_rows/pallas_call | solution.py:377
  160.6 0.0 collective-permute-done
  160.6 1.7 %copy.20 = bf16[1,256,512]{2,1,0:T(8,128)(2,1)} copy(bf16[1,256,512]{2,1,0:T(8,128)(2,1)} %bitcast.21) | data formatting | bytes 524288
  162.3 1.7 %copy.21 = bf16[1,256,512]{2,1,0:T(8,128)(2,1)} copy(bf16[1,256,512]{2,1,0:T(8,128)(2,1)} %bitcast.20) | data formatting | bytes 524288
  163.9 0.0 copy-start.1
  163.9 0.0 copy-start
  163.9 1.3 copy.22
  165.3 0.0 copy-done.1
  165.3 0.7 copy.23
  166.0 0.0 copy-done
  166.0 0.7 copy.24
Async XLA Ops:
  99.7 60.9 %collective-permute-start = (bf16[256,4096]{1,0:T(8,128)(2,1)}, bf16[256,4096]{1,0:T(8,128)(2,1)S(1)}, u32[]{:S(2)}, u32[]{:S(2)}) collective-permute-start(bf16[256,4096]{1,0:T(8,128)(2,1)} %get-tuple-element.16), channel_id=1, source_target_pairs={{8,0},{16,8},{24,16},{9,1},{17,9},{25,17},{10,2},{18,10},{26,18},{... | collective-permute-start | bytes 6291464 | tf_op jit(solution)/shard_map/ppermute | solution.py:392
  163.9 1.3 copy-start.1
  163.9 2.0 %copy-start = (bf16[256,512]{1,0:T(8,128)(2,1)S(1)}, bf16[256,512]{1,0:T(8,128)(2,1)}, u32[]{:S(2)}) copy-start(bf16[256,512]{1,0:T(8,128)(2,1)} %get-tuple-element.21) | copy-start | bytes 786436
